TPU v7x, 256 devices: a whole 4x4x8 slice. The times are simulated.
256 devices in a mesh: dp: 32 (over x_lo, z, core), tensor: 8 (over x_hi, y).
Axes of the slice: x: 4 (x_hi: 2, x_lo: 2; x = x_hi * 2 + x_lo), y: 4, z: 8, core: 2. Of those that a mesh axis runs over, the one named last changes fastest.
Arguments:
- averaged_picture_features: bfloat16 [65536, 1536], P(('dp', 'tensor')), may hold values from -6 to 6
- averaged_caption_features: bfloat16 [65536, 1536], P(('dp', 'tensor')), may hold values from -6 to 6
- picture_projector_weights_array: bfloat16 [1536, 1536], P(None, 'tensor'), may hold values from -0.00390625 to 0.00390625
- caption_projector_weights: bfloat16 [1536, 1536], P(None, 'tensor'), may hold values from -0.00390625 to 0.00390625
- sharpness_coefficient: float32 [1], replicated, may hold values from 5 to 15
- offset_term: float32 [1], replicated, may hold values from -3 to -1
- step_mate_bitflags: int32 [4], replicated, may hold values from 0 to 4, as said below
Outputs:
- grad_image: float32 [65536, 1536], P(('dp', 'tensor'))
- grad_text: float32 [65536, 1536], P(('dp', 'tensor'))
- row_loss: float32 [65536], P(('dp', 'tensor'))
Inputs may be any that keep to these rules, and one draw needn't show every extreme that they name: `step_mate_bitflags`: 4 distinct values; 0 and 4 are always among them.
All inputs are finite; a program needn't handle non-finite values.
Results may differ from a plain program's by a relative error of at most 0.0003.
Values may be sent and summed in bfloat16 or wider, within the bound.
A program may use at most 128 MiB of HBM per device.

v0:
```python
import jax
import jax.numpy as jnp
from jax import lax
from jax.sharding import PartitionSpec as P

highest = lax.Precision.HIGHEST


def from_partner(value, axis, apart):
    mask = 2**apart
    pairs = [(source, source ^ mask) for source in range(lax.axis_size(axis))]
    return lax.ppermute(value, axis, pairs)


def normalize(embedding):
    inverse = lax.rsqrt(jnp.sum(embedding * embedding, axis=-1) + 1e-06)
    return (embedding * inverse[..., None], inverse)


def matmul(first, second):
    return jnp.dot(first, second, precision=highest, preferred_element_type=jnp.float32)


def tile_terms(image_side, text_side, similarity_multiplier, logit_bias, labels):
    logits = similarity_multiplier * matmul(image_side, text_side.T) + logit_bias
    signed = labels * logits
    losses = jnp.sum(jax.nn.softplus(-signed), axis=-1)
    weights = -labels * jax.nn.sigmoid(-signed) * similarity_multiplier
    return (losses, weights)


def backward_pass(grad_unit, embedding, inverse):
    radial = jnp.sum(embedding * grad_unit, axis=-1)
    return inverse[:, None] * grad_unit - (inverse**3 * radial)[:, None] * embedding


def select_partner(arrived, hop_list, wanted):
    result = jnp.zeros_like(arrived[hop_list[0]])
    for hop_bit in hop_list:
        result = jnp.where(wanted == hop_bit, arrived[hop_bit], result)
    return result


def body(
    averaged_picture_features,
    averaged_caption_features,
    picture_projector_weights_array,
    caption_projector_weights,
    sharpness_coefficient,
    offset_term,
    step_mate_bitflags,
):
    features = jnp.stack([averaged_picture_features, averaged_caption_features])
    head_pair = jnp.stack([picture_projector_weights_array, caption_projector_weights])
    projected = jnp.einsum(
        "prw,pwe->pre",
        lax.all_gather(features, "tensor", axis=1, tiled=True),
        head_pair,
        preferred_element_type=jnp.float32,
    )
    embeds = lax.all_to_all(projected, "tensor", split_axis=1, concat_axis=2, tiled=True)
    unit_embeds, inverse = normalize(embeds)
    image_unit = unit_embeds[0]
    text_unit = unit_embeds[1]
    similarity_multiplier = sharpness_coefficient[0]
    logit_bias = offset_term[0]
    pair_rows = image_unit.shape[0]
    own_labels = jnp.where(jnp.eye(pair_rows, dtype=bool), 1.0, -1.0).astype(jnp.float32)
    other_labels = -jnp.ones((pair_rows, pair_rows), jnp.float32)
    losses, weights = tile_terms(
        image_unit, text_unit, similarity_multiplier, logit_bias, own_labels
    )
    grad_image_unit = matmul(weights, text_unit)
    grad_text_unit = matmul(weights.T, image_unit)
    dp_levels = lax.axis_size("dp").bit_length() - 1
    hop_list = list(range(dp_levels))
    rounds = step_mate_bitflags.shape[0]
    arrived = {}
    for hop_bit in hop_list:
        arrived[hop_bit] = from_partner(text_unit, "dp", hop_bit)
    returned = []
    for round_index in range(rounds):
        partner = select_partner(arrived, hop_list, step_mate_bitflags[round_index])
        tile_loss, tile_weights = tile_terms(
            image_unit, partner, similarity_multiplier, logit_bias, other_labels
        )
        losses = losses + tile_loss
        grad_image_unit = grad_image_unit + matmul(tile_weights, partner)
        returned.append(matmul(tile_weights.T, image_unit))
    outgoing = {}
    for hop_bit in hop_list:
        picked = jnp.zeros_like(text_unit)
        for round_index in range(rounds):
            picked = jnp.where(
                step_mate_bitflags[round_index] == hop_bit, returned[round_index], picked
            )
        outgoing[hop_bit] = picked
    for hop_bit in hop_list:
        grad_text_unit = grad_text_unit + from_partner(outgoing[hop_bit], "dp", hop_bit)
    grad_image = backward_pass(grad_image_unit, embeds[0], inverse[0])
    grad_text = backward_pass(grad_text_unit, embeds[1], inverse[1])
    row_loss = losses / ((rounds + 1) * pair_rows)
    return (grad_image, grad_text, row_loss)


def solution(mesh):
    placed = (
        P(("dp", "tensor"), None),
        P(("dp", "tensor"), None),
        P(None, "tensor"),
        P(None, "tensor"),
        P(),
        P(),
        P(),
    )
    return jax.shard_map(
        body,
        mesh=mesh,
        in_specs=placed,
        out_specs=(P(("dp", "tensor"), None), P(("dp", "tensor"), None), P(("dp", "tensor"))),
        check_vma=False,
    )
```

profile of v0, /device:TPU:1, one launch (start us, length us, event | category | flops | bytes accessed | tf_op | source)
XLA Modules:
  0.0 565.0 jit_solution(3561871623589206689)
XLA Ops:
  7.2 2.7 pad_maximum_fusion
  9.9 154.7 %all-gather.2.cloned.1.call-done = bf16[2,2048,1536]{2,1,0:T(8,128)(2,1)} async-done(((bf16[2,256,1536]{2,1,0:T(8,128)(2,1)}), bf16[2,2048,1536]{2,1,0:T(8,128)(2,1)}) %all-gather.2.cloned.1.call-update) | async-done | bytes 12582928 | tf_op jit(solution)/shard_map/all_gather | solution.py:57
  164.6 7.5 %fusion.6 = f32[2,2048,192]{1,2,0:T(8,128)S(1)} fusion(bf16[2,2048,1536]{2,1,0:T(8,128)(2,1)} %all-gather.2.cloned.1.call-done, bf16[1,1536,192]{1,2,0:T(8,128)(2,1)} %bitcast.105, bf16[1,1536,192]{1,2,0:T(8,128)(2,1)} %bitcast.106), kind=kOutput, calls=%fused_computation.27 | convolution fusion | flops 2416508928 | bytes 16908288 | tf_op jit(solution)/shard_map/prw,pwe->pre/dot_general | solution.py:55
  172.0 4.4 copy.25
  176.5 53.6 %all_to_all.18 = f32[2,2048,192]{2,0,1:T(2,128)} all-to-all(f32[2,2048,192]{2,0,1:T(2,128)} %copy.25), channel_id=1, replica_groups=mesh['dp'=32,'tensor'=8] {'tensor'}, dimensions={1} | all-to-all | bytes 6291456 | tf_op jit(solution)/shard_map/all_to_all | solution.py:61
  230.1 3.8 copy.35
  233.9 7.3 %copy.36 = f32[2,8,256,192]{2,3,1,0:T(8,128)} copy(f32[2,8,256,192]{3,0,2,1:T(2,128)} %bitcast.98) | data formatting | bytes 6291456 | tf_op jit(solution)/shard_map/all_to_all | solution.py:61
  241.2 3.6 copy.28
  245.0 1.6 copy-done.4
  246.9 1.3 slice_bitcast_fusion
  248.2 0.9 collective-permute-start
  249.1 5.5 collective-permute-start.1
  255.4 4.2 collective-permute-start.4
  259.6 0.7 fusion.49
  274.7 1.3 fusion.47
  276.1 1.6 copy.29
  277.7 3.0 copy.30
  280.7 3.1 copy.32
  283.8 3.0 copy.33
  286.8 1.6 fusion.26
  288.4 1.5 fusion.45
  289.9 8.4 %collective-permute-done.1 = f32[256,1536]{1,0:T(8,128)} collective-permute-done((f32[256,1536]{1,0:T(8,128)}, f32[256,1536]{1,0:T(8,128)}, u32[]{:S(2)}, u32[]{:S(2)}) %collective-permute-start.1) | collective-permute-done | bytes 1572896 | tf_op jit(solution)/shard_map/ppermute | solution.py:12
  298.3 93.1 %collective-permute-done.2 = f32[256,1536]{1,0:T(8,128)} collective-permute-done((f32[256,1536]{1,0:T(8,128)}, f32[256,1536]{1,0:T(8,128)}, u32[]{:S(2)}, u32[]{:S(2)}) %collective-permute-start.2) | collective-permute-done | bytes 1572896 | tf_op jit(solution)/shard_map/ppermute | solution.py:12
  391.4 4.2 select_select_fusion.7
  395.6 1.6 fusion.30
  397.2 1.5 fusion.32
  398.7 4.2 select_select_fusion.8
  402.9 1.8 fusion.29
  404.7 1.5 fusion.22
  406.2 1.6 fusion.28
  407.8 1.5 fusion.21
  409.3 1.6 fusion.27
  411.0 1.5 fusion.20
  412.5 2.0 select_select_fusion.4
  414.5 0.7 collective-permute-start.9
  415.2 0.9 collective-permute-start.8
  416.1 0.7 select_select_fusion.3
  417.0 2.4 collective-permute-start.6
  419.3 1.6 collective-permute-start.5
  421.0 1.5 convolution_add_fusion.2
  422.5 1.5 fusion.31
  424.0 2.1 multiply_reduce_fusion.2
  426.6 1.4 multiply_subtract_fusion.1
  428.0 22.0 %collective-permute-done.9 = f32[256,1536]{1,0:T(8,128)S(1)} collective-permute-done((f32[256,1536]{1,0:T(8,128)S(1)}, f32[256,1536]{1,0:T(8,128)S(1)}, u32[]{:S(2)}, u32[]{:S(2)}) %collective-permute-start.9) | collective-permute-done | bytes 1572896 | tf_op jit(solution)/shard_map/ppermute | solution.py:12
  450.1 36.3 %collective-permute-done.8 = f32[256,1536]{1,0:T(8,128)S(1)} collective-permute-done((f32[256,1536]{1,0:T(8,128)S(1)}, f32[256,1536]{1,0:T(8,128)S(1)}, u32[]{:S(2)}, u32[]{:S(2)}) %collective-permute-start.8) | collective-permute-done | bytes 1572896 | tf_op jit(solution)/shard_map/ppermute | solution.py:12
  486.4 67.8 %collective-permute-done.7 = f32[256,1536]{1,0:T(8,128)S(1)} collective-permute-done((f32[256,1536]{1,0:T(8,128)S(1)}, f32[256,1536]{1,0:T(8,128)S(1)}, u32[]{:S(2)}, u32[]{:S(2)}) %collective-permute-start.7) | collective-permute-done | bytes 1572896 | tf_op jit(solution)/shard_map/ppermute | solution.py:12
  554.2 2.3 multiply_reduce_fusion.1
  556.5 1.4 multiply_subtract_fusion
  (28 shorter events, 2.1 us)
Async XLA Ops:
  7.2 157.4 %all-gather.2.cloned.1.call-start = ((), (), s32[]{:S(2)}) async-start(), calls=%async_computation.1 | async-start | bytes 14155776 | tf_op jit(solution)/shard_map/all_gather | solution.py:57
  233.9 10.8 %copy-start = (f32[2,8,256,192]{2,1,3,0:T(8,128)}, f32[2,8,256,192]{2,1,3,0:T(8,128)S(1)}, u32[]{:S(2)}) copy-start(f32[2,8,256,192]{2,1,3,0:T(8,128)S(1)} %copy.35) | copy-start | bytes 9437188
  244.8 1.9 copy-start.4
  246.7 12.9 %copy-start.5 = (s32[4]{0:T(128)S(1)}, s32[4]{0:T(128)}, u32[]{:S(2)}) copy-start(s32[4]{0:T(128)} %param.13) | copy-start | bytes 52
  246.9 27.8 %copy-start.1 = (f32[2,8,256,192]{2,1,3,0:T(8,128)S(1)}, f32[2,8,256,192]{2,1,3,0:T(8,128)}, u32[]{:S(2)}) copy-start(f32[2,8,256,192]{2,1,3,0:T(8,128)} %copy-done) | copy-start | bytes 9437188
  248.2 41.7 %collective-permute-start = (f32[256,1536]{1,0:T(8,128)}, f32[256,1536]{1,0:T(8,128)}, u32[]{:S(2)}, u32[]{:S(2)}) collective-permute-start(f32[256,1536]{1,0:T(8,128)} %slice_bitcast_fusion), channel_id=1, source_target_pairs={{0,128},{8,136},{16,144},{24,152},{32,160},{40,168},{48,176},{56,1... | collective-permute-start | bytes 4718600 | tf_op jit(solution)/shard_map/ppermute | solution.py:12
  249.1 49.3 %collective-permute-start.1 = (f32[256,1536]{1,0:T(8,128)}, f32[256,1536]{1,0:T(8,128)}, u32[]{:S(2)}, u32[]{:S(2)}) collective-permute-start(f32[256,1536]{1,0:T(8,128)} %slice_bitcast_fusion), channel_id=1, source_target_pairs={{0,64},{8,72},{16,80},{24,88},{32,96},{40,104},{48,112},{56,120},{... | collective-permute-start | bytes 4718600 | tf_op jit(solution)/shard_map/ppermute | solution.py:12
  254.5 136.9 %collective-permute-start.2 = (f32[256,1536]{1,0:T(8,128)}, f32[256,1536]{1,0:T(8,128)}, u32[]{:S(2)}, u32[]{:S(2)}) collective-permute-start(f32[256,1536]{1,0:T(8,128)} %slice_bitcast_fusion), channel_id=1, source_target_pairs={{0,32},{8,40},{16,48},{24,56},{32,0},{40,8},{48,16},{56,24},{64,96... | collective-permute-start | bytes 4718600 | tf_op jit(solution)/shard_map/ppermute | solution.py:12
  255.0 136.4 %collective-permute-start.3 = (f32[256,1536]{1,0:T(8,128)}, f32[256,1536]{1,0:T(8,128)}, u32[]{:S(2)}, u32[]{:S(2)}) collective-permute-start(f32[256,1536]{1,0:T(8,128)} %slice_bitcast_fusion), channel_id=1, source_target_pairs={{0,16},{8,24},{16,0},{24,8},{32,48},{40,56},{48,32},{56,40},{64,80... | collective-permute-start | bytes 4718600 | tf_op jit(solution)/shard_map/ppermute | solution.py:12
  255.4 136.0 %collective-permute-start.4 = (f32[256,1536]{1,0:T(8,128)}, f32[256,1536]{1,0:T(8,128)}, u32[]{:S(2)}, u32[]{:S(2)}) collective-permute-start(f32[256,1536]{1,0:T(8,128)} %slice_bitcast_fusion), channel_id=1, source_target_pairs={{0,8},{8,0},{16,24},{24,16},{32,40},{40,32},{48,56},{56,48},{64,72... | collective-permute-start | bytes 4718600 | tf_op jit(solution)/shard_map/ppermute | solution.py:12
  414.5 35.6 %collective-permute-start.9 = (f32[256,1536]{1,0:T(8,128)S(1)}, f32[256,1536]{1,0:T(8,128)S(1)}, u32[]{:S(2)}, u32[]{:S(2)}) collective-permute-start(f32[256,1536]{1,0:T(8,128)S(1)} %get-tuple-element.8), channel_id=1, source_target_pairs={{0,128},{8,136},{16,144},{24,152},{32,160},{40,168},{48,176},{56,1... | collective-permute-start | bytes 4718600 | tf_op jit(solution)/shard_map/ppermute | solution.py:12
  415.2 71.2 %collective-permute-start.8 = (f32[256,1536]{1,0:T(8,128)S(1)}, f32[256,1536]{1,0:T(8,128)S(1)}, u32[]{:S(2)}, u32[]{:S(2)}) collective-permute-start(f32[256,1536]{1,0:T(8,128)S(1)} %get-tuple-element.9), channel_id=1, source_target_pairs={{0,64},{8,72},{16,80},{24,88},{32,96},{40,104},{48,112},{56,120},{... | collective-permute-start | bytes 4718600 | tf_op jit(solution)/shard_map/ppermute | solution.py:12
  416.9 137.3 %collective-permute-start.7 = (f32[256,1536]{1,0:T(8,128)S(1)}, f32[256,1536]{1,0:T(8,128)S(1)}, u32[]{:S(2)}, u32[]{:S(2)}) collective-permute-start(f32[256,1536]{1,0:T(8,128)S(1)} %get-tuple-element.11), channel_id=1, source_target_pairs={{0,32},{8,40},{16,48},{24,56},{32,0},{40,8},{48,16},{56,24},{64,96... | collective-permute-start | bytes 4718600 | tf_op jit(solution)/shard_map/ppermute | solution.py:12
  417.0 137.2 %collective-permute-start.6 = (f32[256,1536]{1,0:T(8,128)S(1)}, f32[256,1536]{1,0:T(8,128)S(1)}, u32[]{:S(2)}, u32[]{:S(2)}) collective-permute-start(f32[256,1536]{1,0:T(8,128)S(1)} %get-tuple-element.10), channel_id=1, source_target_pairs={{0,16},{8,24},{16,0},{24,8},{32,48},{40,56},{48,32},{56,40},{64,80... | collective-permute-start | bytes 4718600 | tf_op jit(solution)/shard_map/ppermute | solution.py:12
  419.3 134.9 %collective-permute-start.5 = (f32[256,1536]{1,0:T(8,128)S(1)}, f32[256,1536]{1,0:T(8,128)S(1)}, u32[]{:S(2)}, u32[]{:S(2)}) collective-permute-start(f32[256,1536]{1,0:T(8,128)S(1)} %get-tuple-element.7), channel_id=1, source_target_pairs={{0,8},{8,0},{16,24},{24,16},{32,40},{40,32},{48,56},{56,48},{64,72... | collective-permute-start | bytes 4718600 | tf_op jit(solution)/shard_map/ppermute | solution.py:12
  422.5 1.5 copy-start.2
  426.6 127.6 %copy-start.3 = (f32[256,1536]{1,0:T(8,128)S(1)}, f32[256,1536]{1,0:T(8,128)}, u32[]{:S(2)}) copy-start(f32[256,1536]{1,0:T(8,128)} %copy.33) | copy-start | bytes 4718596
Sparse Core Ops, SparseCore 0:
  11.2 153.3 all-gather.1
where the time goes:
time: 570 us; the launch traced here: 565 us
  waiting for transfers between devices  382 us (67%)
  blocking collectives  53.6 us (9%)
  local copies, waits for them, and re-layouts  34.7 us (6%)
  matrix products  32.5 us (6%)
  between operations  28.9 us (5%)
  starting transfers between devices  17.1 us (3%)
  other arithmetic  15.7 us (3%)
    ppermute x10, waiting for transfers between devices, from_partner(): return lax.ppermute(value, axis, pairs)  228 us
    all_gather x1, waiting for transfers between devices, body(): lax.all_gather(features, 'tensor', axis=1, tiled=True)  155 us
    all_to_all x1, blocking collectives, body(): lax.all_to_all(projected, 'tensor', split_axis=1, concat_axis=2, tiled=True)  53.6 us
    dot_general x15, matrix products, matmul(): jnp.dot(first, second, precision=highest, preferred_element_type=jnp.floa...  25.1 us
    ppermute x10, starting transfers between devices, from_partner(): return lax.ppermute(value, axis, pairs)  17.1 us
    all_to_all x3, local copies, waits for them, and re-layouts, body(): lax.all_to_all(projected, 'tensor', split_axis=1, concat_axis=2, tiled=True)  14.6 us
  transfers between devices with their start and end apart: 11, of which 6 were waited for; matrix products, arithmetic and copies ran while one was open for 4% of the time, Pallas kernels for 0%

commit v1 on v0

v1 whole, which is shorter than its diff:
```python
import functools

import jax
import jax.numpy as jnp
from jax import lax
from jax.experimental import pallas as pl
from jax.experimental.pallas import tpu as pltpu
from jax.sharding import PartitionSpec as P

MESH = pl.DeviceIdType.MESH
OWN, CORE, X_LO, Z1, Z2 = 0, 1, 2, 3, 4
CHUNKS = 8
PIECES = 2 * CHUNKS
STEP = 3
AHEAD = 4


def flip(value, bit):
    size = 2**bit
    return value + size * (1 - 2 * ((value // size) % 2))


def dot(first, second):
    return jnp.dot(first, second, preferred_element_type=jnp.float32)


def dot_t(first, second):
    return lax.dot_general(
        first, second, (((1,), (1,)), ((), ())), preferred_element_type=jnp.float32
    )


def split(value):
    high = value.astype(jnp.bfloat16)
    low = (value - high.astype(jnp.float32)).astype(jnp.bfloat16)
    return high, low


def kernel(
    skip,
    image_ref,
    text_ref,
    image_w_ref,
    text_w_ref,
    scale_ref,
    bias_ref,
    grad_image_ref,
    grad_text_ref,
    loss_ref,
    feat,
    weights,
    emb,
    inv,
    inv_rows,
    totals,
    a_hi,
    a_lo,
    sums,
    hi,
    lo,
    loss_acc,
    out,
    own_sem,
    send_sem,
    recv_sem,
    z1_send,
    z1_recv,
    z2_send,
    z2_recv,
    w_send,
    w_recv,
    inv_send,
    inv_recv,
    out_sem,
):
    rows, width = image_ref.shape
    shard = image_w_ref.shape[0]
    dp = lax.axis_index("dp")
    tensor = lax.axis_index("tensor")
    core = dp % 2
    y = tensor % 4
    x_hi = tensor // 4

    def at(x_side, y_place):
        return x_side * 4 + (y_place + 4) % 4

    if skip == 1:
        z1_dp, far_dp = flip(dp, 2), flip(dp, 3)
        hop_dp = flip(flip(dp, 2), 3)
    elif skip == 2:
        z1_dp, far_dp = flip(dp, 1), flip(dp, 3)
        hop_dp = flip(flip(dp, 1), 3)
    else:
        z1_dp, far_dp = flip(dp, 1), flip(dp, 2)
        hop_dp = far_dp
    core_to = (flip(dp, 0), tensor)
    x_to = (flip(dp, 4), tensor)
    cross_to = (flip(dp, 4), at(1 - x_hi, y))
    up_to = (dp, at(x_hi, y + 1))
    down_to = (dp, at(x_hi, y - 1))
    z1_to = (z1_dp, tensor)
    hop_to = (hop_dp, tensor)
    far_to = (far_dp, tensor)

    barrier = pltpu.get_barrier_semaphore()
    peers = [core_to, x_to, cross_to, up_to, down_to, z1_to, hop_to]
    if skip != 3:
        peers.append(far_to)
    for peer in peers:
        pl.semaphore_signal(barrier, inc=1, device_id=peer, device_id_type=MESH)
    pl.semaphore_wait(barrier, len(peers))

    def remote(src, dst, send, recv, to):
        return pltpu.make_async_remote_copy(
            src_ref=src, dst_ref=dst, send_sem=send, recv_sem=recv, device_id=to, device_id_type=MESH
        )

    chunk_rows = rows // CHUNKS
    inputs = (image_ref, text_ref)
    def rows_of(j):
        return pl.ds(pl.multiple_of((j % CHUNKS) * chunk_rows, chunk_rows), chunk_rows)

    def z1_copy(j, source=None):
        landing = feat.at[Z1, j // CHUNKS, rows_of(j)]
        return remote(
            landing if source is None else source, landing, z1_send.at[j], z1_recv.at[j], z1_to
        )

    def z2_copy(j, source=None):
        source = feat.at[Z1, j // CHUNKS, rows_of(j)] if source is None else source
        landing = feat.at[Z2, j // CHUNKS, rows_of(j)]
        return remote(source, landing, z2_send.at[j], z2_recv.at[j], hop_to)

    def send_chunk(j, _, source=None):
        source = feat.at[OWN, j // CHUNKS, rows_of(j)] if source is None else source
        z1_copy(j, source).start()
        if skip == 3:
            z2_copy(j, source).start()
        return 0

    at_once = AHEAD if skip == 1 else PIECES
    lax.fori_loop(
        0, min(at_once, CHUNKS), lambda j, _: send_chunk(j, 0, image_ref.at[rows_of(j)]), 0
    )
    lax.fori_loop(
        CHUNKS, max(at_once, CHUNKS), lambda j, _: send_chunk(j, 0, text_ref.at[rows_of(j)]), 0
    )

    w_inputs = (image_w_ref, text_w_ref)
    shard_rows = (0, shard)
    first_rows = (0, shard // 2)
    second_rows = (shard // 2, shard // 2)
    below, above, opposite = at(x_hi, y - 1), at(x_hi, y + 1), at(x_hi, y + 2)
    cross = at(1 - x_hi, y)
    cross_below, cross_above, cross_opposite = (
        at(1 - x_hi, y - 1),
        at(1 - x_hi, y + 1),
        at(1 - x_hi, y + 2),
    )

    def place(kind, slot, part):
        offset = pl.multiple_of(slot * shard + part[0], shard // 2)
        return weights.at[kind, pl.ds(offset, part[1])]

    def shard_copy(kind, slot, part, send, recv, to):
        ref = place(kind, slot, part)
        return remote(ref, ref, w_send.at[send], w_recv.at[recv], to)

    def own_shard_copy(kind, number, to):
        return remote(
            w_inputs[kind],
            place(kind, tensor, shard_rows),
            w_send.at[number],
            w_recv.at[number],
            to,
        )

    own_targets = (up_to, down_to, cross_to)
    for kind in range(2):

        @pl.when(core == kind)
        def _():
            for number, to in enumerate(own_targets):
                own_shard_copy(kind, number, to).start()

    def whole_copy(kind, base, n, to):
        return remote(
            inputs[kind], feat.at[base, kind], send_sem.at[n], recv_sem.at[n], to
        )

    whole = [
        whole_copy(0, X_LO, 2, x_to),
        whole_copy(1, X_LO, 3, x_to),
        whole_copy(0, CORE, 0, core_to),
        whole_copy(1, CORE, 1, core_to),
    ]
    for copy in whole:
        copy.start()
    own = [pltpu.make_async_copy(inputs[k], feat.at[OWN, k], own_sem.at[k]) for k in range(2)]
    for kind in range(2):
        own.append(
            pltpu.make_async_copy(
                w_inputs[kind], place(kind, tensor, shard_rows), own_sem.at[2 + kind]
            )
        )
    for copy in own:
        copy.start()

    def send(slot, part, number, to):
        shard_copy(core, slot, part, number, number, to).start()

    def swap(number, slot):
        send(slot, shard_rows, 8 + number, core_to)

    def arrived(slot, part, recv):
        shard_copy(core, slot, part, recv, recv, core_to).wait_recv()

    def swapped(number, slot):
        shard_copy(1 - core, slot, shard_rows, 8 + number, 8 + number, core_to).wait_recv()

    def relay(first, last):
        def one(j, _):
            z1_copy(j).wait_recv()
            if skip != 3:
                z2_copy(j).start()
            if skip == 1:

                @pl.when(j + AHEAD < PIECES)
                def _():
                    send_chunk(j + AHEAD, 0)

            return 0

        lax.fori_loop(first, last, one, 0)

    def wait_z2(first, last):
        def one(j, _):
            z2_copy(j).wait_recv()
            return 0

        lax.fori_loop(first, last, one, 0)

    def early(first, last):
        if skip != 3:
            relay(first, last)

    tiles = width // 256

    def tile(n):
        return slice(n * 256, (n + 1) * 256)

    def over_tiles(body, carry):
        def several(m, carry):
            for k in range(STEP):
                carry = body(pl.ds(pl.multiple_of((m * STEP + k) * 256, 256), 256), carry)
            return carry

        return lax.fori_loop(0, tiles // STEP, several, carry)

    scale = scale_ref[0]
    bias = bias_ref[0]
    loss_acc[...] = jnp.zeros_like(loss_acc)
    sums[...] = jnp.zeros_like(sums)

    totals[...] = jnp.zeros_like(totals)
    out[...] = jnp.zeros_like(out)
    for copy in own:
        copy.wait()

    def group(g, _):
        @pl.when(g == 0)
        def _():
            early(0, 3)
            arrived(below, shard_rows, 0)
            arrived(above, shard_rows, 1)
            send(below, first_rows, 3, up_to)
            send(above, second_rows, 4, down_to)
            arrived(cross, shard_rows, 2)
            swap(0, below)
            swap(1, above)
            swap(2, cross)
            early(3, 4)
            arrived(opposite, first_rows, 3)
            arrived(opposite, second_rows, 4)
            send(cross, shard_rows, 5, up_to)
            send(cross, shard_rows, 6, down_to)
            send(opposite, shard_rows, 7, cross_to)
            swap(3, opposite)
            early(4, 5)
            swapped(0, below)
            swapped(1, above)
            swapped(3, opposite)

        @pl.when(g == 1)
        def _():
            early(6, 7)
            arrived(cross_below, shard_rows, 5)
            swap(4, cross_below)
            arrived(cross_above, shard_rows, 6)
            swap(5, cross_above)
            arrived(cross_opposite, shard_rows, 7)
            swap(6, cross_opposite)
            early(7, 8)
            swapped(2, cross)
            swapped(4, cross_below)
            swapped(5, cross_above)
            swapped(6, cross_opposite)

        side = x_hi + g * (1 - 2 * x_hi)
        begin = pl.multiple_of(side * (width // 2), width // 2)

        def embed(kind, _):
            def one(m, total):
                for k in range(STEP):
                    part = pl.ds(pl.multiple_of(begin + (m * STEP + k) * 256, 256), 256)
                    value = dot_t(feat[OWN, kind], weights[kind, part, :])
                    emb[kind, :, part] = value
                    square = value * value
                    total = total + square[:, 0:128] + square[:, 128:256]
                return total

            totals[kind] = lax.fori_loop(0, tiles // 2 // STEP, one, totals[kind])
            return 0

        lax.fori_loop(0, 2, embed, 0)
        early(5 + 3 * g, 6 + 3 * g)

        def through(kind, _):
            half = pl.ds(begin, width // 2)
            hi_half, lo_half = split(emb[1 - kind, :, half])

            def back(part, carry):
                right = weights[kind, half, part]
                out[kind, :, part] += dot(hi_half, right) + dot(lo_half, right)
                return carry

            over_tiles(back, 0)
            return 0

        lax.fori_loop(0, 2, through, 0)
        return 0

    lax.fori_loop(0, 2, group, 0)

    def inv_copy(n, base, to):
        return remote(inv_rows.at[OWN], inv_rows.at[base], inv_send.at[n], inv_recv.at[n], to)

    inv_copies = [
        inv_copy(2, Z1, z1_to),
        inv_copy(3, Z2, far_to),
        inv_copy(0, CORE, core_to),
        inv_copy(1, X_LO, x_to),
    ]

    for kind in range(2):
        inverse = lax.rsqrt(jnp.sum(totals[kind], axis=-1, keepdims=True) + 1e-06)
        wide = jnp.broadcast_to(inverse, (rows, 128))
        inv[kind] = wide
        inv_rows[OWN, kind] = wide.T[0:8]
    for copy in inv_copies:
        copy.start()

    def queries(kind, _):
        factor = inv[1 - kind][:, 0:1]
        for n in range(tiles):
            a_hi[kind, :, tile(n)], a_lo[kind, :, tile(n)] = split(out[kind, :, tile(n)] * factor)
        return 0

    lax.fori_loop(0, 2, queries, 0)

    def terms(block, kind):
        keys = feat[block, kind]
        inner = dot_t(a_hi[kind], keys) + dot_t(a_lo[kind], keys)
        factor = scale * inv_rows[block, kind, 0:1, :]
        logit = inner * factor + bias
        row = lax.broadcasted_iota(jnp.int32, logit.shape, 0)
        column = lax.broadcasted_iota(jnp.int32, logit.shape, 1)
        own_rows = jnp.where(block == OWN, rows, 0)
        sign = jnp.where((row == column) & (row < own_rows), -1.0, 1.0).astype(jnp.float32)
        signed = sign * logit
        coef = (sign * factor) / (1.0 + jnp.exp(-signed))

        @pl.when(kind == 1)
        def _():
            loss = jnp.maximum(signed, 0.0) + jnp.log1p(jnp.exp(-jnp.abs(signed)))
            loss_acc[...] += loss[:, 0:128] + loss[:, 128:256]

        coef_hi, coef_lo = split(coef)

        def add(part, carry):
            key = feat[block, kind, :, part]
            sums[kind, :, part] += dot(coef_hi, key) + dot(coef_lo, key)
            return carry

        over_tiles(add, 0)

    def finish(kind):
        query = 1 - kind
        for n in range(tiles):
            hi[:, tile(n)], lo[:, tile(n)] = split(sums[kind, :, tile(n)])

        def back(part, radial):
            right = weights[kind, part, :]
            value = dot_t(hi[...], right) + dot_t(lo[...], right)
            out[query, :, part] = value
            product = value * emb[query, :, part]
            return radial + product[:, 0:128] + product[:, 128:256]

        radial = over_tiles(back, jnp.zeros((rows, 128), jnp.float32))
        inverse = inv[query][:, 0:1]
        factor = inverse * inverse * inverse * jnp.sum(radial, axis=-1, keepdims=True)
        for n in range(tiles):
            out[query, :, tile(n)] = (
                inverse * out[query, :, tile(n)] - factor * emb[query, :, tile(n)]
            )

    first_end = 8

    def chunks_by(n):
        if skip == 3:
            return jnp.where(n < 6, 0, CHUNKS)
        return jnp.where(n < 0, 9, 9 + (n + 1) // 3)

    out_refs = (grad_image_ref, grad_text_ref)
    out_copies = [
        pltpu.make_async_copy(out.at[k], out_refs[k], out_sem.at[k]) for k in range(2)
    ]

    def step(n, _):
        relay(chunks_by(n - 1), chunks_by(n))

        @pl.when((n == first_end) | (n == 10))
        def _():
            finish(n // 10)

        for query, when in enumerate((10, first_end)):

            @pl.when(n == when)
            def _(query=query):
                out_copies[query].start()

        @pl.when(n == first_end)
        def _():
            relay(chunks_by(n), PIECES)

        @pl.when(n == 2)
        def _():
            for copy in whole[2:] + inv_copies[2:]:
                copy.wait_recv()

        @pl.when(n == 4)
        def _():
            for copy in whole[:2]:
                copy.wait_recv()

        @pl.when(n == 6)
        def _():
            for copy in inv_copies[:2]:
                copy.wait_recv()

        @pl.when(n == 7)
        def _():
            wait_z2(0, CHUNKS)

        @pl.when(n == 9)
        def _():
            wait_z2(CHUNKS, PIECES)

        block_z = Z1 + n % 2
        kind_z = (n - 6) // 2

        @pl.when(n < 10)
        def _():
            terms(jnp.where(n < 6, n // 2, block_z), jnp.where(n < 6, n % 2, kind_z))

        return 0

    lax.fori_loop(0, 11, step, 0)
    loss_ref[...] = jnp.sum(loss_acc[...].T, axis=0, keepdims=True) / (5 * rows)

    for copy in whole + inv_copies:
        copy.wait_send()

    def sent(j, _):
        z1_copy(j).wait_send()
        z2_copy(j).wait_send()
        return 0

    lax.fori_loop(0, PIECES, sent, 0)
    for copy in out_copies:
        copy.wait()
    for number, to in enumerate(own_targets):
        own_shard_copy(0, number, to).wait_send()
    for slot, part, number in (
        (below, first_rows, 3),
        (above, second_rows, 4),
        (cross, shard_rows, 5),
        (cross, shard_rows, 6),
        (opposite, shard_rows, 7),
    ):
        shard_copy(core, slot, part, number, number, core_to).wait_send()
    for number, slot in enumerate(
        (below, above, cross, opposite, cross_below, cross_above, cross_opposite)
    ):
        shard_copy(core, slot, shard_rows, 8 + number, 8 + number, core_to).wait_send()


def run(skip, image, text, image_w, text_w, scale, bias):
    rows, width = image.shape
    dma = pltpu.SemaphoreType.DMA
    f32, bf16 = jnp.float32, jnp.bfloat16
    any_spec = pl.BlockSpec(memory_space=pl.ANY)
    vmem = pl.BlockSpec(memory_space=pltpu.VMEM)
    smem = pl.BlockSpec(memory_space=pltpu.SMEM)
    grad_image, grad_text, loss = pl.pallas_call(
        functools.partial(kernel, skip),
        out_shape=(
            jax.ShapeDtypeStruct((rows, width), f32),
            jax.ShapeDtypeStruct((rows, width), f32),
            jax.ShapeDtypeStruct((1, rows), f32),
        ),
        in_specs=[any_spec, any_spec, any_spec, any_spec, smem, smem],
        out_specs=(any_spec, any_spec, vmem),
        scratch_shapes=[
            pltpu.VMEM((5, 2, rows, width), bf16),
            pltpu.VMEM((2, width, width), bf16),
            pltpu.VMEM((2, rows, width), f32),
            pltpu.VMEM((2, rows, 128), f32),
            pltpu.VMEM((5, 2, 8, rows), f32),
            pltpu.VMEM((2, rows, 128), f32),
            pltpu.VMEM((2, rows, width), bf16),
            pltpu.VMEM((2, rows, width), bf16),
            pltpu.VMEM((2, rows, width), f32),
            pltpu.VMEM((rows, width), bf16),
            pltpu.VMEM((rows, width), bf16),
            pltpu.VMEM((rows, 128), f32),
            pltpu.VMEM((2, rows, width), f32),
            dma((4,)),
            dma((4,)),
            dma((4,)),
            dma((2 * CHUNKS,)),
            dma((2 * CHUNKS,)),
            dma((2 * CHUNKS,)),
            dma((2 * CHUNKS,)),
            dma((15,)),
            dma((15,)),
            dma((4,)),
            dma((4,)),
            dma((2,)),
        ],
        compiler_params=pltpu.CompilerParams(
            collective_id=skip, has_side_effects=True, vmem_limit_bytes=48 * 2**20
        ),
    )(image, text, image_w.T, text_w.T, scale, bias)
    return grad_image, grad_text, loss


def body(image, text, image_w, text_w, scale, bias, flags):
    skip = 10 - jnp.sum(flags)
    grad_image, grad_text, loss = lax.switch(
        skip - 1,
        [functools.partial(run, 1), functools.partial(run, 2), functools.partial(run, 3)],
        image,
        text,
        image_w,
        text_w,
        scale,
        bias,
    )
    return grad_image, grad_text, loss.reshape(loss.shape[1])


def solution(mesh):
    placed = (
        P(("dp", "tensor"), None),
        P(("dp", "tensor"), None),
        P(None, "tensor"),
        P(None, "tensor"),
        P(),
        P(),
        P(),
    )
    return jax.shard_map(
        body,
        mesh=mesh,
        in_specs=placed,
        out_specs=(P(("dp", "tensor"), None), P(("dp", "tensor"), None), P(("dp", "tensor"))),
        check_vma=False,
    )
```

time: 570 us -> 109 us (0.19)
  waiting for transfers between devices: 382 us -> 0 us
  Pallas kernels: 0 us -> 103 us
  blocking collectives: 53.6 us -> 0 us
  matrix products: 32.5 us -> 0 us
  local copies, waits for them, and re-layouts: 34.7 us -> 2.85 us
  between operations: 28.9 us -> 1.29 us
  starting transfers between devices: 17.1 us -> 0 us
  other arithmetic: 15.7 us -> 1.29 us
    ppermute x10 -> x0, waiting for transfers between devices: 228 us -> none  [from_partner(): return lax.ppermute(value, axis, pairs)]
    all_gather x1 -> x0, waiting for transfers between devices: 155 us -> none  [body(): lax.all_gather(features, 'tensor', axis=1, tiled=True)]
    pallas_call x0 -> x1, Pallas kernels: none -> 103 us  [run(): pl.pallas_call(functools.partial(kernel, skip), out_shape=(jax.ShapeDtype...]
    all_to_all x1 -> x0, blocking collectives: 53.6 us -> none  [body(): lax.all_to_all(projected, 'tensor', split_axis=1, concat_axis=2, tiled=True)]
    dot_general x16 -> x0, matrix products: 32.5 us -> none  [the longest x15 25.1 us: matmul(): jnp.dot(first, second, precision=highest, preferred_element_type=jnp.floa...]
    ppermute x10 -> x0, starting transfers between devices: 17.1 us -> none  [from_partner(): return lax.ppermute(value, axis, pairs)]
    all_to_all x3 -> x0, local copies, waits for them, and re-layouts: 14.6 us -> none  [body(): lax.all_to_all(projected, 'tensor', split_axis=1, concat_axis=2, tiled=True)]
    select_n x3 -> x0, other arithmetic: 9.16 us -> none  [the longest x2 8.42 us: select_partner(): result = jnp.where(wanted == hop_bit, arrived[hop_bit], result)]
  transfers between devices with their start and end apart: 11 -> 0, of which waited for: 6 -> 0; matrix products, arithmetic and copies ran while one was open for 4% -> 0% of each run, Pallas kernels for 0% -> 0%
where the time goes in v1:
time: 109 us
  Pallas kernels  103 us (94%)
  local copies, waits for them, and re-layouts  2.85 us (3%)
  other arithmetic  1.29 us (1%)
  between operations  1.29 us (1%)
    pallas_call x1, Pallas kernels, run(): pl.pallas_call(functools.partial(kernel, skip), out_shape=(jax.ShapeDtype...  103 us
    unnamed x3, local copies, waits for them, and re-layouts  2.85 us

profile of v1, /device:TPU:1, one launch (start us, length us, event | category | flops | bytes accessed | tf_op | source)
XLA Modules:
  0.0 109.2 jit_solution(12182043932968976915)
XLA Ops:
  0.6 1.3 %reduce_sum.9 = s32[]{:T(128)} reduce(s32[4]{0:T(128)} %param.16, s32[]{:T(128)} %constant.3.clone.1), dimensions={0}, to_apply=%region_0.0 | reduce | flops 3 | bytes 24 | tf_op jit(solution)/shard_map/reduce_sum | solution.py:559
  2.6 103.8 %conditional.1 = (f32[256,1536]{1,0:T(8,128)S(1)}, f32[256,1536]{1,0:T(8,128)S(1)}, f32[256]{0:T(256)S(1)}) conditional(s32[]{:T(128)} %clamp.3, (bf16[1536,192]{0,1:T(8,128)(2,1)}, bf16[1536,192]{0,1:T(8,128)(2,1)}, bf16[256,1536]{1,0:T(8,128)(2,1)}, bf16[256,1536]{1,0:T(8,128)(2,1)}, f32[1]{0:T(128)}, ...), branch_computations={%region_1.0_spmd, %region_2.0_spmd, %region_3.0_spmd} | conditional | bytes 24 | solution.py:560
  2.6 103.4 %branch_1_fun.1 = (f32[256,1536]{1,0:T(8,128)S(1)}, f32[256,1536]{1,0:T(8,128)S(1)}, f32[1,256]{1,0:T(1,128)S(1)}) custom-call(bf16[256,1536]{1,0:T(8,128)(2,1)} %get-tuple-element.55.image_ref, bf16[256,1536]{1,0:T(8,128)(2,1)} %get-tuple-element.56.text_ref, bf16[192,1536]{1,0:T(8,128)(2,1)} %bitcast.10, bf16[192,1536]{1,0:T(8,128)(2,1)} %bitcast.13, ...), custom_call_target="tpu_custom_call" | custom-call | tf_op jit(solution)/shard_map/cond/branch_1_fun/pallas_call | solution.py:515
  106.4 1.1 %copy.25 = f32[256,1536]{1,0:T(8,128)} copy(f32[256,1536]{1,0:T(8,128)S(1)} %get-tuple-element.89) | data formatting | bytes 3145728
  107.5 1.1 %copy.26 = f32[256,1536]{1,0:T(8,128)} copy(f32[256,1536]{1,0:T(8,128)S(1)} %get-tuple-element.90) | data formatting | bytes 3145728
  108.7 0.6 copy.27

commit v2 on v1

--- a/solution.py
+++ b/solution.py
@@ -9,6 +9,7 @@
 
 MESH = pl.DeviceIdType.MESH
 OWN, CORE, X_LO, Z1, Z2 = 0, 1, 2, 3, 4
+PARTS = 2
 CHUNKS = 8
 PIECES = 2 * CHUNKS
 STEP = 3
@@ -53,6 +54,8 @@
     inv,
     inv_rows,
     totals,
+    key_inv,
+    radial_sums,
     a_hi,
     a_lo,
     sums,
@@ -120,31 +123,35 @@
     def rows_of(j):
         return pl.ds(pl.multiple_of((j % CHUNKS) * chunk_rows, chunk_rows), chunk_rows)
 
+    per_part = CHUNKS // PARTS
+    part_rows = rows // PARTS
+
+    def landing(far, j):
+        k = j - CHUNKS
+        image = (6 + far) * rows + j * chunk_rows
+        text = 8 * rows + (2 * (k // per_part) + far) * part_rows
+        text = text + (k % per_part) * chunk_rows
+        start = jnp.where(j < CHUNKS, image, text)
+        return feat.at[pl.ds(pl.multiple_of(start, chunk_rows), chunk_rows)]
+
     def z1_copy(j, source=None):
-        landing = feat.at[Z1, j // CHUNKS, rows_of(j)]
+        place = landing(0, j)
         return remote(
-            landing if source is None else source, landing, z1_send.at[j], z1_recv.at[j], z1_to
+            place if source is None else source, place, z1_send.at[j], z1_recv.at[j], z1_to
         )
 
     def z2_copy(j, source=None):
-        source = feat.at[Z1, j // CHUNKS, rows_of(j)] if source is None else source
-        landing = feat.at[Z2, j // CHUNKS, rows_of(j)]
-        return remote(source, landing, z2_send.at[j], z2_recv.at[j], hop_to)
+        source = landing(0, j) if source is None else source
+        return remote(source, landing(1, j), z2_send.at[j], z2_recv.at[j], hop_to)
 
     def send_chunk(j, _, source=None):
-        source = feat.at[OWN, j // CHUNKS, rows_of(j)] if source is None else source
+        source = feat.at[pl.ds(pl.multiple_of(j * chunk_rows, chunk_rows), chunk_rows)] if source is None else source
         z1_copy(j, source).start()
         if skip == 3:
             z2_copy(j, source).start()
         return 0
 
-    at_once = AHEAD if skip == 1 else PIECES
-    lax.fori_loop(
-        0, min(at_once, CHUNKS), lambda j, _: send_chunk(j, 0, image_ref.at[rows_of(j)]), 0
-    )
-    lax.fori_loop(
-        CHUNKS, max(at_once, CHUNKS), lambda j, _: send_chunk(j, 0, text_ref.at[rows_of(j)]), 0
-    )
+    lax.fori_loop(0, AHEAD, lambda j, _: send_chunk(j, 0, image_ref.at[rows_of(j)]), 0)
 
     w_inputs = (image_w_ref, text_w_ref)
     shard_rows = (0, shard)
@@ -183,9 +190,12 @@
             for number, to in enumerate(own_targets):
                 own_shard_copy(kind, number, to).start()
 
+    def piece(n):
+        return feat.at[pl.ds(pl.multiple_of(n * rows, rows), rows)]
+
     def whole_copy(kind, base, n, to):
         return remote(
-            inputs[kind], feat.at[base, kind], send_sem.at[n], recv_sem.at[n], to
+            inputs[kind], piece(2 * base + kind), send_sem.at[n], recv_sem.at[n], to
         )
 
     whole = [
@@ -196,7 +206,7 @@
     ]
     for copy in whole:
         copy.start()
-    own = [pltpu.make_async_copy(inputs[k], feat.at[OWN, k], own_sem.at[k]) for k in range(2)]
+    own = [pltpu.make_async_copy(inputs[k], piece(k), own_sem.at[k]) for k in range(2)]
     for kind in range(2):
         own.append(
             pltpu.make_async_copy(
@@ -223,11 +233,10 @@
             z1_copy(j).wait_recv()
             if skip != 3:
                 z2_copy(j).start()
-            if skip == 1:
-
-                @pl.when(j + AHEAD < PIECES)
-                def _():
-                    send_chunk(j + AHEAD, 0)
+
+            @pl.when(j + AHEAD < PIECES)
+            def _():
+                send_chunk(j + AHEAD, 0)
 
             return 0
 
@@ -239,10 +248,6 @@
             return 0
 
         lax.fori_loop(first, last, one, 0)
-
-    def early(first, last):
-        if skip != 3:
-            relay(first, last)
 
     tiles = width // 256
 
@@ -270,7 +275,7 @@
     def group(g, _):
         @pl.when(g == 0)
         def _():
-            early(0, 3)
+            relay(0, 3)
             arrived(below, shard_rows, 0)
             arrived(above, shard_rows, 1)
             send(below, first_rows, 3, up_to)
@@ -279,28 +284,28 @@
             swap(0, below)
             swap(1, above)
             swap(2, cross)
-            early(3, 4)
+            relay(3, 4)
             arrived(opposite, first_rows, 3)
             arrived(opposite, second_rows, 4)
             send(cross, shard_rows, 5, up_to)
             send(cross, shard_rows, 6, down_to)
             send(opposite, shard_rows, 7, cross_to)
             swap(3, opposite)
-            early(4, 5)
+            relay(4, 5)
             swapped(0, below)
             swapped(1, above)
             swapped(3, opposite)
 
         @pl.when(g == 1)
         def _():
-            early(6, 7)
+            relay(6, 7)
             arrived(cross_below, shard_rows, 5)
             swap(4, cross_below)
             arrived(cross_above, shard_rows, 6)
             swap(5, cross_above)
             arrived(cross_opposite, shard_rows, 7)
             swap(6, cross_opposite)
-            early(7, 8)
+            relay(7, 8)
             swapped(2, cross)
             swapped(4, cross_below)
             swapped(5, cross_above)
@@ -313,7 +318,7 @@
             def one(m, total):
                 for k in range(STEP):
                     part = pl.ds(pl.multiple_of(begin + (m * STEP + k) * 256, 256), 256)
-                    value = dot_t(feat[OWN, kind], weights[kind, part, :])
+                    value = dot_t(piece(kind)[...], weights[kind, part, :])
                     emb[kind, :, part] = value
                     square = value * value
                     total = total + square[:, 0:128] + square[:, 128:256]
@@ -323,7 +328,7 @@
             return 0
 
         lax.fori_loop(0, 2, embed, 0)
-        early(5 + 3 * g, 6 + 3 * g)
+        relay(5 + 3 * g, 6 + 3 * g)
 
         def through(kind, _):
             half = pl.ds(begin, width // 2)
@@ -368,15 +373,15 @@
 
     lax.fori_loop(0, 2, queries, 0)
 
-    def terms(block, kind):
-        keys = feat[block, kind]
+    def coefs(keys, kind, inverses, diagonal):
+        keys = keys[...]
         inner = dot_t(a_hi[kind], keys) + dot_t(a_lo[kind], keys)
-        factor = scale * inv_rows[block, kind, 0:1, :]
+        factor = scale * inverses
         logit = inner * factor + bias
         row = lax.broadcasted_iota(jnp.int32, logit.shape, 0)
         column = lax.broadcasted_iota(jnp.int32, logit.shape, 1)
-        own_rows = jnp.where(block == OWN, rows, 0)
-        sign = jnp.where((row == column) & (row < own_rows), -1.0, 1.0).astype(jnp.float32)
+        label_rows = jnp.where(diagonal, rows, 0)
+        sign = jnp.where((row == column) & (row < label_rows), -1.0, 1.0).astype(jnp.float32)
         signed = sign * logit
         coef = (sign * factor) / (1.0 + jnp.exp(-signed))
 
@@ -385,63 +390,71 @@
             loss = jnp.maximum(signed, 0.0) + jnp.log1p(jnp.exp(-jnp.abs(signed)))
             loss_acc[...] += loss[:, 0:128] + loss[:, 128:256]
 
-        coef_hi, coef_lo = split(coef)
-
+        return split(coef)
+
+    def add_terms(keys, kind, coef_hi, coef_lo):
         def add(part, carry):
-            key = feat[block, kind, :, part]
+            key = keys[:, part]
             sums[kind, :, part] += dot(coef_hi, key) + dot(coef_lo, key)
             return carry
 
         over_tiles(add, 0)
 
-    def finish(kind):
-        query = 1 - kind
+    def out_of_space(kind):
         for n in range(tiles):
             hi[:, tile(n)], lo[:, tile(n)] = split(sums[kind, :, tile(n)])
 
         def back(part, radial):
             right = weights[kind, part, :]
             value = dot_t(hi[...], right) + dot_t(lo[...], right)
-            out[query, :, part] = value
-            product = value * emb[query, :, part]
+            out[1 - kind, :, part] = value
+            product = value * emb[1 - kind, :, part]
             return radial + product[:, 0:128] + product[:, 128:256]
 
-        radial = over_tiles(back, jnp.zeros((rows, 128), jnp.float32))
+        radial_sums[...] = over_tiles(back, jnp.zeros((rows, 128), jnp.float32))
+
+    out_refs = (grad_image_ref, grad_text_ref)
+    out_copies = [pltpu.make_async_copy(out.at[k], out_refs[k], out_sem.at[k]) for k in range(2)]
+
+    def finish(query):
         inverse = inv[query][:, 0:1]
-        factor = inverse * inverse * inverse * jnp.sum(radial, axis=-1, keepdims=True)
+        radial = jnp.sum(radial_sums[...], axis=-1, keepdims=True)
+        factor = inverse * inverse * inverse * radial
         for n in range(tiles):
             out[query, :, tile(n)] = (
                 inverse * out[query, :, tile(n)] - factor * emb[query, :, tile(n)]
             )
-
-    first_end = 8
+        for k in range(2):
+
+            @pl.when(query == k)
+            def _(k=k):
+                out_copies[k].start()
+
+    before_finish = 14
 
     def chunks_by(n):
-        if skip == 3:
-            return jnp.where(n < 6, 0, CHUNKS)
-        return jnp.where(n < 0, 9, 9 + (n + 1) // 3)
-
-    out_refs = (grad_image_ref, grad_text_ref)
-    out_copies = [
-        pltpu.make_async_copy(out.at[k], out_refs[k], out_sem.at[k]) for k in range(2)
-    ]
+        return jnp.where(n < 0, 9, jnp.where(n < 8, 9 + (n + 1) // 2, jnp.where(n < 9, 15, PIECES)))
+
+    def key_norms(keys, kind):
+        def one(part, total):
+            value = dot_t(keys[...], weights[kind, part, :])
+            square = value * value
+            return total + square[:, 0:128] + square[:, 128:256]
+
+        total = over_tiles(one, jnp.zeros((rows, 128), jnp.float32))
+        inverse = lax.rsqrt(jnp.sum(total, axis=-1, keepdims=True) + 1e-06)
+        key_inv[...] = jnp.broadcast_to(inverse, (rows, 128)).T[0:8]
+
+    def last_inverses():
+        for copy in inv_copies[:2]:
+            copy.wait_recv()
+        for k, block in enumerate((Z1, Z2)):
+            key_inv[:, k * part_rows : (k + 1) * part_rows] = inv_rows[
+                block, 1, :, rows - part_rows : rows
+            ]
 
     def step(n, _):
-        relay(chunks_by(n - 1), chunks_by(n))
-
-        @pl.when((n == first_end) | (n == 10))
-        def _():
-            finish(n // 10)
-
-        for query, when in enumerate((10, first_end)):
-
-            @pl.when(n == when)
-            def _(query=query):
-                out_copies[query].start()
-
-        @pl.when(n == first_end)
-        def _():
-            relay(chunks_by(n), PIECES)
+        relay(jnp.where(n == 8, before_finish, chunks_by(n - 1)), chunks_by(n))
 
         @pl.when(n == 2)
         def _():
@@ -453,29 +466,43 @@
             for copy in whole[:2]:
                 copy.wait_recv()
 
-        @pl.when(n == 6)
-        def _():
-            for copy in inv_copies[:2]:
-                copy.wait_recv()
-
         @pl.when(n == 7)
         def _():
             wait_z2(0, CHUNKS)
 
+        @pl.when(n >= 8)
+        def _():
+            wait_z2(CHUNKS + (n - 8) * per_part, CHUNKS + (n - 7) * per_part)
+
+        kind = jnp.where(n < 6, n % 2, n // 8)
+        keys = piece(n)
+
+        @pl.when((n >= 6) & (n < 9))
+        def _():
+            key_norms(keys, kind)
+
         @pl.when(n == 9)
         def _():
-            wait_z2(CHUNKS, PIECES)
-
-        block_z = Z1 + n % 2
-        kind_z = (n - 6) // 2
-
-        @pl.when(n < 10)
-        def _():
-            terms(jnp.where(n < 6, n // 2, block_z), jnp.where(n < 6, n % 2, kind_z))
-
+            last_inverses()
+
+        known = inv_rows[jnp.minimum(n // 2, X_LO), kind, 0:1, :]
+        inverses = jnp.where(n < 6, known, key_inv[0:1, :])
+        coef_hi, coef_lo = coefs(keys, kind, inverses, n < 2)
+        add_terms(keys, kind, coef_hi, coef_lo)
         return 0
 
-    lax.fori_loop(0, 11, step, 0)
+    def phase(kind, _):
+        lax.fori_loop(8 * kind, 8 + 2 * kind, step, 0)
+
+        @pl.when(kind == 0)
+        def _():
+            relay(chunks_by(7), before_finish)
+
+        out_of_space(kind)
+        finish(1 - kind)
+        return 0
+
+    lax.fori_loop(0, 2, phase, 0)
     loss_ref[...] = jnp.sum(loss_acc[...].T, axis=0, keepdims=True) / (5 * rows)
 
     for copy in whole + inv_copies:
@@ -522,12 +549,14 @@
         in_specs=[any_spec, any_spec, any_spec, any_spec, smem, smem],
         out_specs=(any_spec, any_spec, vmem),
         scratch_shapes=[
-            pltpu.VMEM((5, 2, rows, width), bf16),
+            pltpu.VMEM((10 * rows, width), bf16),
             pltpu.VMEM((2, width, width), bf16),
             pltpu.VMEM((2, rows, width), f32),
             pltpu.VMEM((2, rows, 128), f32),
             pltpu.VMEM((5, 2, 8, rows), f32),
             pltpu.VMEM((2, rows, 128), f32),
+            pltpu.VMEM((8, rows), f32),
+            pltpu.VMEM((rows, 128), f32),
             pltpu.VMEM((2, rows, width), bf16),
             pltpu.VMEM((2, rows, width), bf16),
             pltpu.VMEM((2, rows, width), f32),

time: 109 us -> 91.7 us (0.84)
  Pallas kernels: 103 us -> 85.7 us
    pallas_call x1, Pallas kernels: 103 us -> 85.7 us  [run(): pl.pallas_call(functools.partial(kernel, skip), out_shape=(jax.ShapeDtype...]
where the time goes in v2:
time: 91.7 us; the launch traced here: 91.6 us
  Pallas kernels  85.7 us (93%)
  local copies, waits for them, and re-layouts  2.85 us (3%)
  other arithmetic  1.29 us (1%)
  between operations  1.29 us (1%)
    pallas_call x1, Pallas kernels, run(): pl.pallas_call(functools.partial(kernel, skip), out_shape=(jax.ShapeDtype...  85.7 us
    unnamed x3, local copies, waits for them, and re-layouts  2.85 us

profile of v2, /device:TPU:1, one launch (start us, length us, event | category | flops | bytes accessed | tf_op | source)
XLA Modules:
  0.0 91.6 jit_solution(10190248854118185034)
XLA Ops:
  0.6 1.3 %reduce_sum.9 = s32[]{:T(128)} reduce(s32[4]{0:T(128)} %param.16, s32[]{:T(128)} %constant.3.clone.1), dimensions={0}, to_apply=%region_0.0 | reduce | flops 3 | bytes 24 | tf_op jit(solution)/shard_map/reduce_sum | solution.py:588
  2.6 86.1 %conditional.1 = (f32[256,1536]{1,0:T(8,128)S(1)}, f32[256,1536]{1,0:T(8,128)S(1)}, f32[256]{0:T(256)S(1)}) conditional(s32[]{:T(128)} %clamp.3, (bf16[1536,192]{0,1:T(8,128)(2,1)}, bf16[1536,192]{0,1:T(8,128)(2,1)}, bf16[256,1536]{1,0:T(8,128)(2,1)}, bf16[256,1536]{1,0:T(8,128)(2,1)}, f32[1]{0:T(128)}, ...), branch_computations={%region_1.0_spmd, %region_2.0_spmd, %region_3.0_spmd} | conditional | bytes 24 | solution.py:589
  2.8 85.7 %branch_2_fun.1 = (f32[256,1536]{1,0:T(8,128)S(1)}, f32[256,1536]{1,0:T(8,128)S(1)}, f32[1,256]{1,0:T(1,128)S(1)}) custom-call(bf16[256,1536]{1,0:T(8,128)(2,1)} %get-tuple-element.64.image_ref, bf16[256,1536]{1,0:T(8,128)(2,1)} %get-tuple-element.65.text_ref, bf16[192,1536]{1,0:T(8,128)(2,1)} %bitcast.11, bf16[192,1536]{1,0:T(8,128)(2,1)} %bitcast.14, ...), custom_call_target="tpu_custom_call" | custom-call | tf_op jit(solution)/shard_map/cond/branch_2_fun/pallas_call | solution.py:542
  88.7 1.1 %copy.25 = f32[256,1536]{1,0:T(8,128)} copy(f32[256,1536]{1,0:T(8,128)S(1)} %get-tuple-element.89) | data formatting | bytes 3145728
  89.8 1.1 %copy.26 = f32[256,1536]{1,0:T(8,128)} copy(f32[256,1536]{1,0:T(8,128)S(1)} %get-tuple-element.90) | data formatting | bytes 3145728
  91.0 0.6 copy.27

commit v3 on v2

--- a/solution.py
+++ b/solution.py
@@ -13,7 +13,8 @@
 CHUNKS = 8
 PIECES = 2 * CHUNKS
 STEP = 3
-AHEAD = 4
+AHEAD = {1: 3, 2: 4, 3: 4}
+PASSED = {1: (3, 4, 5, 6, 7, 8, 9), 2: (3, 5, 6, 7, 8, 9, 10), 3: (3, 4, 5, 6, 7, 8, 9)}
 
 
 def flip(value, bit):
@@ -74,7 +75,6 @@
     w_recv,
     inv_send,
     inv_recv,
-    out_sem,
 ):
     rows, width = image_ref.shape
     shard = image_w_ref.shape[0]
@@ -151,7 +151,9 @@
             z2_copy(j, source).start()
         return 0
 
-    lax.fori_loop(0, AHEAD, lambda j, _: send_chunk(j, 0, image_ref.at[rows_of(j)]), 0)
+    ahead = AHEAD[skip]
+    passed = PASSED[skip]
+    lax.fori_loop(0, ahead, lambda j, _: send_chunk(j, 0, image_ref.at[rows_of(j)]), 0)
 
     w_inputs = (image_w_ref, text_w_ref)
     shard_rows = (0, shard)
@@ -234,9 +236,9 @@
             if skip != 3:
                 z2_copy(j).start()
 
-            @pl.when(j + AHEAD < PIECES)
+            @pl.when(j + ahead < PIECES)
             def _():
-                send_chunk(j + AHEAD, 0)
+                send_chunk(j + ahead, 0)
 
             return 0
 
@@ -275,7 +277,7 @@
     def group(g, _):
         @pl.when(g == 0)
         def _():
-            relay(0, 3)
+            relay(0, passed[0])
             arrived(below, shard_rows, 0)
             arrived(above, shard_rows, 1)
             send(below, first_rows, 3, up_to)
@@ -284,28 +286,28 @@
             swap(0, below)
             swap(1, above)
             swap(2, cross)
-            relay(3, 4)
+            relay(passed[0], passed[1])
             arrived(opposite, first_rows, 3)
             arrived(opposite, second_rows, 4)
             send(cross, shard_rows, 5, up_to)
             send(cross, shard_rows, 6, down_to)
             send(opposite, shard_rows, 7, cross_to)
             swap(3, opposite)
-            relay(4, 5)
+            relay(passed[1], passed[2])
             swapped(0, below)
             swapped(1, above)
             swapped(3, opposite)
 
         @pl.when(g == 1)
         def _():
-            relay(6, 7)
+            relay(passed[3], passed[4])
             arrived(cross_below, shard_rows, 5)
             swap(4, cross_below)
             arrived(cross_above, shard_rows, 6)
             swap(5, cross_above)
             arrived(cross_opposite, shard_rows, 7)
             swap(6, cross_opposite)
-            relay(7, 8)
+            relay(passed[4], passed[5])
             swapped(2, cross)
             swapped(4, cross_below)
             swapped(5, cross_above)
@@ -328,7 +330,15 @@
             return 0
 
         lax.fori_loop(0, 2, embed, 0)
-        relay(5 + 3 * g, 6 + 3 * g)
+
+        @pl.when(g == 0)
+        def _():
+            relay(passed[2], passed[3])
+
+        @pl.when(g == 1)
+        def _():
+            relay(passed[5], passed[6])
+
 
         def through(kind, _):
             half = pl.ds(begin, width // 2)
@@ -414,26 +424,26 @@
         radial_sums[...] = over_tiles(back, jnp.zeros((rows, 128), jnp.float32))
 
     out_refs = (grad_image_ref, grad_text_ref)
-    out_copies = [pltpu.make_async_copy(out.at[k], out_refs[k], out_sem.at[k]) for k in range(2)]
 
     def finish(query):
         inverse = inv[query][:, 0:1]
         radial = jnp.sum(radial_sums[...], axis=-1, keepdims=True)
         factor = inverse * inverse * inverse * radial
-        for n in range(tiles):
-            out[query, :, tile(n)] = (
-                inverse * out[query, :, tile(n)] - factor * emb[query, :, tile(n)]
-            )
         for k in range(2):
 
             @pl.when(query == k)
-            def _(k=k):
-                out_copies[k].start()
+            def _(out_ref=out_refs[k]):
+                for n in range(tiles):
+                    out_ref[:, tile(n)] = (
+                        inverse * out[query, :, tile(n)] - factor * emb[query, :, tile(n)]
+                    )
 
     before_finish = 14
 
     def chunks_by(n):
-        return jnp.where(n < 0, 9, jnp.where(n < 8, 9 + (n + 1) // 2, jnp.where(n < 9, 15, PIECES)))
+        middle = jnp.minimum(passed[6] + (n + 1) // 2, before_finish)
+        middle = jnp.where(n < 0, passed[6], middle)
+        return jnp.where(n < 8, middle, jnp.where(n < 9, 15, PIECES))
 
     def key_norms(keys, kind):
         def one(part, total):
@@ -514,8 +524,6 @@
         return 0
 
     lax.fori_loop(0, PIECES, sent, 0)
-    for copy in out_copies:
-        copy.wait()
     for number, to in enumerate(own_targets):
         own_shard_copy(0, number, to).wait_send()
     for slot, part, number in (
@@ -547,7 +555,7 @@
             jax.ShapeDtypeStruct((1, rows), f32),
         ),
         in_specs=[any_spec, any_spec, any_spec, any_spec, smem, smem],
-        out_specs=(any_spec, any_spec, vmem),
+        out_specs=(vmem, vmem, vmem),
         scratch_shapes=[
             pltpu.VMEM((10 * rows, width), bf16),
             pltpu.VMEM((2, width, width), bf16),
@@ -575,7 +583,6 @@
             dma((15,)),
             dma((4,)),
             dma((4,)),
-            dma((2,)),
         ],
         compiler_params=pltpu.CompilerParams(
             collective_id=skip, has_side_effects=True, vmem_limit_bytes=48 * 2**20

time: 91.7 us -> 102 us (1.11)
  the two profiles are of different devices: /device:TPU:1 before, /device:TPU:48 now
where the time goes in v3:
time: 102 us
  Pallas kernels  96.3 us (94%)
  local copies, waits for them, and re-layouts  2.85 us (3%)
  other arithmetic  1.29 us (1%)
  between operations  1.29 us (1%)
    pallas_call x1, Pallas kernels, run(): pl.pallas_call(functools.partial(kernel, skip), out_shape=(jax.ShapeDtype...  96.3 us
    unnamed x3, local copies, waits for them, and re-layouts  2.85 us

profile of v3, /device:TPU:48, one launch (start us, length us, event | category | flops | bytes accessed | tf_op | source)
XLA Modules:
  0.0 102.0 jit_solution(17955284958985866710)
XLA Ops:
  0.6 1.3 %reduce_sum.9 = s32[]{:T(128)} reduce(s32[4]{0:T(128)} %param.16, s32[]{:T(128)} %constant.3.clone.1), dimensions={0}, to_apply=%region_0.0 | reduce | flops 3 | bytes 24 | tf_op jit(solution)/shard_map/reduce_sum | solution.py:595
  2.6 96.5 %conditional.1 = (f32[256,1536]{1,0:T(8,128)S(1)}, f32[256,1536]{1,0:T(8,128)S(1)}, f32[256]{0:T(256)S(1)}) conditional(s32[]{:T(128)} %clamp.3, (bf16[1536,192]{0,1:T(8,128)(2,1)}, bf16[1536,192]{0,1:T(8,128)(2,1)}, bf16[256,1536]{1,0:T(8,128)(2,1)}, bf16[256,1536]{1,0:T(8,128)(2,1)}, f32[1]{0:T(128)}, ...), branch_computations={%region_1.0_spmd, %region_2.0_spmd, %region_3.0_spmd} | conditional | bytes 24 | solution.py:596
  2.6 96.3 %branch_0_fun.1 = (f32[256,1536]{1,0:T(8,128)S(1)}, f32[256,1536]{1,0:T(8,128)S(1)}, f32[1,256]{1,0:T(1,128)S(1)}) custom-call(bf16[256,1536]{1,0:T(8,128)(2,1)} %get-tuple-element.46.image_ref, bf16[256,1536]{1,0:T(8,128)(2,1)} %get-tuple-element.47.text_ref, bf16[192,1536]{1,0:T(8,128)(2,1)} %bitcast.9, bf16[192,1536]{1,0:T(8,128)(2,1)} %bitcast.12, ...), custom_call_target="tpu_custom_call" | custom-call | tf_op jit(solution)/shard_map/cond/branch_0_fun/pallas_call | solution.py:550
  99.1 1.1 %copy.25 = f32[256,1536]{1,0:T(8,128)} copy(f32[256,1536]{1,0:T(8,128)S(1)} %get-tuple-element.89) | data formatting | bytes 3145728
  100.3 1.1 %copy.26 = f32[256,1536]{1,0:T(8,128)} copy(f32[256,1536]{1,0:T(8,128)S(1)} %get-tuple-element.90) | data formatting | bytes 3145728
  101.4 0.6 copy.27

commit v4 on v3

--- a/solution.py
+++ b/solution.py
@@ -13,7 +13,7 @@
 CHUNKS = 8
 PIECES = 2 * CHUNKS
 STEP = 3
-AHEAD = {1: 3, 2: 4, 3: 4}
+AHEAD = {1: 2, 2: 4, 3: 4}
 PASSED = {1: (3, 4, 5, 6, 7, 8, 9), 2: (3, 5, 6, 7, 8, 9, 10), 3: (3, 4, 5, 6, 7, 8, 9)}
 
 
@@ -414,14 +414,15 @@
         for n in range(tiles):
             hi[:, tile(n)], lo[:, tile(n)] = split(sums[kind, :, tile(n)])
 
-        def back(part, radial):
+        radial = jnp.zeros((rows, 128), jnp.float32)
+        for n in range(tiles):
+            part = tile(n)
             right = weights[kind, part, :]
             value = dot_t(hi[...], right) + dot_t(lo[...], right)
             out[1 - kind, :, part] = value
             product = value * emb[1 - kind, :, part]
-            return radial + product[:, 0:128] + product[:, 128:256]
-
-        radial_sums[...] = over_tiles(back, jnp.zeros((rows, 128), jnp.float32))
+            radial = radial + product[:, 0:128] + product[:, 128:256]
+        radial_sums[...] = radial
 
     out_refs = (grad_image_ref, grad_text_ref)
 

time: 102 us -> 97.6 us (0.957)
  the two profiles are of different devices: /device:TPU:48 before, /device:TPU:1 now
where the time goes in v4:
time: 97.6 us; the launch traced here: 99.1 us
  Pallas kernels  92.9 us (95%)
  local copies, waits for them, and re-layouts  2.85 us (3%)
  other arithmetic  1.29 us (1%)
  between operations  1.29 us (1%)
    pallas_call x1, Pallas kernels, run(): pl.pallas_call(functools.partial(kernel, skip), out_shape=(jax.ShapeDtype...  92.9 us
    unnamed x3, local copies, waits for them, and re-layouts  2.85 us

profile of v4, /device:TPU:1, one launch (start us, length us, event | category | flops | bytes accessed | tf_op | source)
XLA Modules:
  0.0 99.1 jit_solution(4622295306743345336)
XLA Ops:
  0.6 1.3 %reduce_sum.9 = s32[]{:T(128)} reduce(s32[4]{0:T(128)} %param.16, s32[]{:T(128)} %constant.3.clone.1), dimensions={0}, to_apply=%region_0.0 | reduce | flops 3 | bytes 24 | tf_op jit(solution)/shard_map/reduce_sum | solution.py:596
  2.6 93.6 %conditional.1 = (f32[256,1536]{1,0:T(8,128)S(1)}, f32[256,1536]{1,0:T(8,128)S(1)}, f32[256]{0:T(256)S(1)}) conditional(s32[]{:T(128)} %clamp.3, (bf16[1536,192]{0,1:T(8,128)(2,1)}, bf16[1536,192]{0,1:T(8,128)(2,1)}, bf16[256,1536]{1,0:T(8,128)(2,1)}, bf16[256,1536]{1,0:T(8,128)(2,1)}, f32[1]{0:T(128)}, ...), branch_computations={%region_1.0_spmd, %region_2.0_spmd, %region_3.0_spmd} | conditional | bytes 24 | solution.py:597
  2.8 92.9 %branch_1_fun.1 = (f32[256,1536]{1,0:T(8,128)S(1)}, f32[256,1536]{1,0:T(8,128)S(1)}, f32[1,256]{1,0:T(1,128)S(1)}) custom-call(bf16[256,1536]{1,0:T(8,128)(2,1)} %get-tuple-element.55.image_ref, bf16[256,1536]{1,0:T(8,128)(2,1)} %get-tuple-element.56.text_ref, bf16[192,1536]{1,0:T(8,128)(2,1)} %bitcast.10, bf16[192,1536]{1,0:T(8,128)(2,1)} %bitcast.13, ...), custom_call_target="tpu_custom_call" | custom-call | tf_op jit(solution)/shard_map/cond/branch_1_fun/pallas_call | solution.py:551
  96.2 1.1 %copy.25 = f32[256,1536]{1,0:T(8,128)} copy(f32[256,1536]{1,0:T(8,128)S(1)} %get-tuple-element.89) | data formatting | bytes 3145728
  97.4 1.1 %copy.26 = f32[256,1536]{1,0:T(8,128)} copy(f32[256,1536]{1,0:T(8,128)S(1)} %get-tuple-element.90) | data formatting | bytes 3145728
  98.5 0.6 copy.27
